TPU v7x, 128 devices: a whole 4x4x4 slice. The times are simulated.
128 devices in a mesh: branch: 2 (over core), section: 2 (over z_hi), patch: 32 (over z_lo, y, x).
Axes of the slice: x: 4, y: 4, z: 4 (z_hi: 2, z_lo: 2; z = z_hi * 2 + z_lo), core: 2. Of those that a mesh axis runs over, the one named last changes fastest.
Arguments:
- stream: bfloat16 [3840, 2560], P('patch'), may hold values from -6 to 6
- token_frame: int32 [3840], P('patch'), may hold values from 0 to 15, never falling along the last dimension, each value on 1 to 480 neighbouring positions
- frame_levels: int32 [16], replicated, may hold values from 0 to 49
- level_table: float32 [50, 7680], replicated, may hold values from -3 to 3
- branch_mod: float32 [2, 7680], P('branch'), may hold values from -2.4 to 2.4
- layer_mod: float32 [2, 7680], P('section'), may hold values from -1.8 to 1.8
- maps: float32 [2, 3, 2560], P('section'), may hold values from -3.6 to 3.6
- stale_kv: bfloat16 [2, 2, 2, 3840, 2560], P('branch', 'section', None, 'patch'), may hold values from -204 to 204
Outputs:
- guided: bfloat16 [3840, 2560], P('patch', 'branch')
- fresh_kv: bfloat16 [2, 2, 2, 3840, 2560], P('branch', 'section', None, 'patch')
Inputs may be any that keep to these rules, and one draw needn't show every extreme that they name: token_frame never falls from one token to the next, and every frame holds between 1 and 480 tokens.
All inputs are finite; a program needn't handle non-finite values.
Results may differ from a plain program's by a relative error of at most 0.025.
Values may be sent and summed in bfloat16 or wider, within the bound.
No kernel may reach another device: no remote copies, remote signals or barrier semaphores. Data moves between devices by JAX's collectives and lax.ppermute only.
A program may use at most 256 MiB of HBM per device.

v0:
```python
import functools
import math

import jax
import jax.numpy as jnp
from jax import lax
from jax.experimental import pallas as pl
from jax.experimental.pallas import tpu as pltpu
from jax.sharding import PartitionSpec as P

HEADS = 20
HEAD_DIM = 128
FRAMES = 16
LEVELS = 50
TOK = 120
THIRD = 40
PATCHES = 32
WIDTH = HEADS * HEAD_DIM
EPSILON = 1e-06
GUIDE = 5.0
BIG = 1e30
PLANE = ("section", "patch")
F32 = jnp.float32
BF16 = jnp.bfloat16
VMEM_BYTES = 56 * 1024 * 1024
PARAMS = pltpu.CompilerParams(vmem_limit_bytes=VMEM_BYTES)

OWN_ROWS = PATCHES * THIRD
TILE = 640
WIDE = 1280
SMALL = 1e-25
FACTOR = HEAD_DIM ** (-0.5) * math.log2(math.e)
CHUNK = 320
MID = 64


def place_of(head, third):
    if head < 16:
        return 4 * head + third
    return 16 * (head - 16) + 4 * third + 3


def dot(a, b, dims):
    return lax.dot_general(a, b, (dims, ((), ())), preferred_element_type=F32)


NN = ((1,), (0,))
NT = ((1,), (1,))
TN = ((0,), (0,))


def split3(v):
    hi = v.astype(BF16).astype(F32)
    mid = (v - hi).astype(BF16).astype(F32)
    low = (v - hi - mid).astype(BF16).astype(F32)
    return hi, mid, low


def turned(rows, third):
    cut = THIRD * third
    return rows if cut == 0 else jnp.concatenate([rows[cut:TOK], rows[:cut]], axis=0)


def pack_kernel(scal, stale, stream, frames, out, aux, frame_row):
    step = pl.program_id(0)
    section = scal[0]

    @pl.when(step == 0)
    def _():
        frame_row[...] = jnp.zeros((8, 128), F32)
        frame_row[0:1, 0:TOK] = frames[...].astype(F32)
        square = jnp.zeros((TOK, 128), F32)
        for head in range(HEADS):
            part = stream[:, 128 * head : 128 * head + 128].astype(F32)
            square = square + part * part
        square = jnp.concatenate([square, jnp.zeros((8, 128), F32)], axis=0)
        total = jnp.sum(square.T, axis=0, keepdims=True)
        r = lax.rsqrt(total * (1.0 / WIDTH) + EPSILON)
        hi, mid, low = split3(jnp.broadcast_to(r, (8, 128)))
        row = lax.broadcasted_iota(jnp.int32, (8, 128), 0)
        lane = lax.broadcasted_iota(jnp.int32, (8, 128), 1)
        a = jnp.where(row == 0, hi, jnp.where(row == 1, mid, jnp.where(row == 2, low, 0.0)))
        a = jnp.where(row == 3, frame_row[0:1, :], a)
        a = jnp.where(lane < TOK, a, 0.0)
        aux[0] = a
        for third in range(1, 3):
            cut = THIRD * third
            t = jnp.where(lane < TOK - cut, pltpu.roll(a, 128 - cut, 1), pltpu.roll(a, TOK - cut, 1))
            aux[third] = jnp.where(lane < TOK, t, 0.0)

    none = jnp.zeros((8, 128), F32)

    def blocks(head):
        cols = pl.ds(pl.multiple_of(head * 128, 128), 128)
        keys = stale[0, :, cols].astype(F32)
        vals = jnp.concatenate([stale[1, :, cols].astype(F32), none], axis=0).T.astype(BF16)
        x = stream[:, cols].astype(F32)
        halves = []
        for third in range(3):
            t = turned(x, third)
            halves.append(jnp.where(section == 0, t[0:64], t[TOK - 64 : TOK]).astype(BF16))
        return keys, vals, halves

    def put(at, keys, vals, x, third):
        out[at, 0:128] = jnp.concatenate([keys, aux[third]], axis=0).astype(BF16)
        out[at, 128:256] = vals
        out[at, 256:CHUNK] = x

    more_keys, more_vals, more_x = blocks(16 + step)
    for y in range(4):
        keys, vals, halves = blocks(4 * step + y)
        for third in range(3):
            put(4 * y + third, keys, vals, halves[third], third)
        put(4 * y + 3, more_keys, more_vals, more_x[y % 3], y % 3)


def pack(section, stale, stream, frames):
    grid = pltpu.PrefetchScalarGridSpec(
        num_scalar_prefetch=1,
        grid=(4,),
        in_specs=[
            pl.BlockSpec((2, TOK, WIDTH), lambda r, s: (0, 0, 0)),
            pl.BlockSpec((TOK, WIDTH), lambda r, s: (0, 0)),
            pl.BlockSpec((1, TOK), lambda r, s: (0, 0)),
        ],
        out_specs=pl.BlockSpec((16, CHUNK, 128), lambda r, s: (r, 0, 0)),
        scratch_shapes=[pltpu.VMEM((3, 8, 128), F32), pltpu.VMEM((8, 128), F32)],
    )
    return pl.pallas_call(
        pack_kernel,
        grid_spec=grid,
        out_shape=jax.ShapeDtypeStruct((64, CHUNK, 128), BF16),
        compiler_params=PARAMS,
        name="pack",
    )(section, stale, stream, frames)


def mod_table(frame_mod, with_scale):
    hi, mid, low = split3(frame_mod)
    table = jnp.concatenate([hi, mid, low, jnp.zeros((16, frame_mod.shape[1]), F32)], axis=0)
    if with_scale:
        row = lax.broadcasted_iota(jnp.int32, (64, 128), 0)
        extra = jnp.where((row >= 48) & (row < 51), 1.0, 0.0)
        table = jnp.concatenate([table, extra], axis=1)
    return table.astype(BF16)


def hot_rows(aux):
    row = lax.broadcasted_iota(jnp.int32, (48, 128), 0)
    hot = jnp.where((row & 15).astype(F32) == aux[3:4, :], 1.0, 0.0)
    return jnp.concatenate([hot, aux, jnp.zeros((8, 128), F32)], axis=0).astype(BF16)


def modulations(kv, table, mods):
    for begin in range(0, PATCHES, 8):
        hot = [hot_rows(kv[0, p, 112:128, :].astype(F32)[8:16]) for p in range(begin, begin + 8)]
        at = slice(begin * 128, begin * 128 + 1024)
        mods[at, 0 : table.shape[1]] = dot(jnp.concatenate(hot, axis=1), table, TN)


def place_pair(t, hids, maps, kv, qa, ka, vt, kf, vh):
    row = lax.broadcasted_iota(jnp.int32, (80, 128), 0)
    col = lax.broadcasted_iota(jnp.int32, (80, 128), 1)
    patch = 2 * t + jnp.where(row >= THIRD, 1, 0)
    at = slice(t * 80, t * 80 + 80)
    q = jnp.concatenate([hid[0:THIRD] for hid in hids], axis=0) * maps[0:1, :]
    qa[at, 0:128] = q.astype(BF16)
    qa[at, 128:256] = jnp.where((col == patch) | (col == PATCHES), 1.0, 0.0).astype(BF16)
    row = lax.broadcasted_iota(jnp.int32, (128, 128), 0)
    col = lax.broadcasted_iota(jnp.int32, (128, 128), 1)
    for half in range(2):
        p = 2 * t + half
        at = slice(p * 128, p * 128 + 128)
        ka[at, 0:128] = kv[0, p, 0:128, :]
        hidden = (col == p) | ((col == PATCHES) & (row >= TOK))
        ka[at, 128:256] = jnp.where(hidden, -BIG, 0.0).astype(BF16)
        vt[0:128, at] = kv[0, p, 128:256, :]
        kf[at, 0:128] = (hids[half] * maps[1:2, :]).astype(BF16)
        hidden = (col <= PATCHES) & ((row >= TOK) | ((col != p) & (col < PATCHES)))
        kf[at, 128:256] = jnp.where(hidden, -BIG, 0.0).astype(BF16)
        vh[at, :] = (hids[half] * maps[2:3, :]).astype(BF16)


def turn_values(vh, vt, vf):
    row = lax.broadcasted_iota(jnp.int32, (128, 128), 0)
    col = lax.broadcasted_iota(jnp.int32, (128, 128), 1)
    unit = jnp.where(row == col, 1.0, 0.0).astype(BF16)
    for begin in range(0, PATCHES * 128, 1024):
        at = slice(begin, begin + 1024)
        vf[0:128, at] = dot(unit, vh[at, :], NT).astype(BF16)
    vt[128:144, :] = jnp.ones((16, PATCHES * 128), BF16)
    vf[128:144, :] = jnp.ones((16, PATCHES * 128), BF16)


def norms(ref):
    ones = jnp.ones((8, 128), BF16)
    parts = []
    for begin in range(0, ref.shape[0], 640 if ref.shape[0] % 1024 else 1024):
        at = slice(begin, begin + (640 if ref.shape[0] % 1024 else 1024))
        v = ref[at, 0:128].astype(F32)
        parts.append(dot(ones, (v * v).astype(BF16), NT))
    return jnp.concatenate(parts, axis=1) * 1.01


def attention(qa, ka, vt, kf, vf, xo, go, sc, pt, result):
    step = 512
    stale = PATCHES * 128
    keys = stale + step
    row = lax.broadcasted_iota(jnp.int32, (128, 256), 0)
    col = lax.broadcasted_iota(jnp.int32, (128, 256), 1)
    unit = jnp.where((row == col) | (row + 128 == col), 1.0, 0.0).astype(BF16)

    def fresh_at(lane):
        low = lane // TILE * (TILE // THIRD) + lane % TILE // 128 * 3
        return pl.ds(low * 128 if isinstance(low, int) else pl.multiple_of(low * 128, 128), step)

    def scores(first, width, begin):
        return dot(ka[pl.ds(begin, step), :], qa[pl.ds(first, width), :], NT)

    def fresh_scores(first, width):
        lanes = [first + i for i in range(0, width, 128)]
        parts = [dot(kf[fresh_at(lane), :], qa[pl.ds(lane, 128), :], NT) for lane in lanes]
        return jnp.concatenate(parts, axis=1)

    def weigh(first, width, begin, s, top):
        weights = jnp.exp2((s - top) * FACTOR).astype(BF16)
        pt[pl.ds(begin, step), pl.ds(first, width)] = weights

    def finish(first, width):
        total = dot(vt[...], pt[0:stale, pl.ds(first, width)], NN)
        lanes = [first + i for i in range(0, width, 128)]
        more = [dot(vf[:, fresh_at(lane)], pt[stale:keys, pl.ds(lane, 128)], NN) for lane in lanes]
        total = total + jnp.concatenate(more, axis=1)
        mean = total[0:128] / total[128:129]
        hi = mean.astype(BF16)
        low = (mean - hi.astype(F32)).astype(BF16)
        for i, lane in enumerate(lanes):
            cols = slice(128 * i, 128 * i + 128)
            attended = dot(unit, jnp.concatenate([hi[:, cols], low[:, cols]], axis=1), NT)
            at = pl.ds(lane, 128)
            result(at, (xo[at, :] + go[at, :] * attended).astype(BF16))
        return jnp.min(total[128:129])

    lane = lax.broadcasted_iota(jnp.int32, (8, stale), 1)
    longest = jnp.where((lane & 127) < TOK, jnp.maximum(norms(ka), norms(kf)), 0.0)
    longest = jnp.max(longest, axis=1, keepdims=True)[0:1]
    bound = jnp.sqrt(norms(qa)[0:1] * longest)
    least = None
    for first in range(0, OWN_ROWS, WIDE):
        top = bound[:, first : first + WIDE]
        for begin in range(0, stale, step):
            weigh(first, WIDE, begin, scores(first, WIDE, begin), top)
        weigh(first, WIDE, stale, fresh_scores(first, WIDE), top)
        here = finish(first, WIDE)
        least = here if least is None else jnp.minimum(least, here)

    @pl.when(jnp.logical_not(least > SMALL))
    def _():
        @pl.loop(0, OWN_ROWS // TILE)
        def _(tile):
            first = pl.multiple_of(tile * TILE, 128)
            s = fresh_scores(first, TILE)
            sc[stale:keys, :] = s

            def one(i, top):
                begin = pl.multiple_of(i * step, step)
                s = scores(first, TILE, begin)
                sc[pl.ds(begin, step), :] = s
                return jnp.maximum(top, jnp.max(s.reshape(step // 8, 8, TILE), axis=0))

            top = lax.fori_loop(0, stale // step, one, jnp.max(s.reshape(step // 8, 8, TILE), axis=0))
            top = jnp.max(top, axis=0, keepdims=True)

            @pl.loop(0, keys // step)
            def _(i):
                begin = pl.multiple_of(i * step, step)
                weigh(first, TILE, begin, sc[pl.ds(begin, step), :], top)

            finish(first, TILE)


def first_kernel(kv, x_rest, frame_mod, maps, x_out, mid, qa, ka, vt, kf, vf, xo, go, sc, pt, mods, vh, sq):
    table = mod_table(frame_mod[...], True)
    gains = maps[...]

    modulations(kv, table, mods)
    for t in range(PATCHES // 2):
        at = slice(t * 80, t * 80 + 80)
        hids, xs, gates = [], [], []
        for half in range(2):
            p = 2 * t + half
            xa = kv[0, p, 256:CHUNK, :].astype(F32)
            xb = x_rest[0, p].astype(F32)[8:64]
            x = jnp.concatenate([xa, xb, jnp.zeros((8, 128), F32)], axis=0)
            m = mods[p * 128 : p * 128 + 128, :]
            hids.append(x * m[:, 384:512] * (1.0 + m[:, 128:256]) + m[:, 0:128])
            xs.append(x[0:THIRD])
            gates.append(m[0:THIRD, 256:384])
        place_pair(t, hids, gains, kv, qa, ka, vt, kf, vh)
        xo[at, :] = jnp.concatenate(xs, axis=0)
        go[at, :] = jnp.concatenate(gates, axis=0)
    turn_values(vh, vt, vf)

    def result(at, value):
        x_out[at, :] = value
        wide = value.astype(F32)
        sq[at, :] = wide * wide

    attention(qa, ka, vt, kf, vf, xo, go, sc, pt, result)
    square = sq[...]
    hi = square.astype(BF16)
    low = (square - hi.astype(F32)).astype(BF16)
    ones = jnp.ones((8, 128), BF16)
    total = dot(ones, hi, NT) + dot(ones, low, NT)
    hi = total.astype(BF16).astype(F32)
    low = total - hi
    rows = [part[0:1, 128 * i : 128 * i + 128] for part in (hi, low) for i in range(10)]
    sums = jnp.concatenate(rows + [jnp.zeros((4, 128), F32)], axis=0)
    for t in range(PATCHES // 2):
        pair = x_out[80 * t : 80 * t + 80, :].astype(F32)
        for half in range(2):
            p = 2 * t + half
            block = jnp.concatenate([pair[THIRD * half : THIRD * half + THIRD], sums], axis=0).astype(BF16)
            mid[p] = block
            mid[PATCHES + p] = block


SCRATCH = [
    pltpu.VMEM((OWN_ROWS, 256), BF16),
    pltpu.VMEM((PATCHES * 128, 256), BF16),
    pltpu.VMEM((144, PATCHES * 128), BF16),
    pltpu.VMEM((PATCHES * 128, 256), BF16),
    pltpu.VMEM((144, PATCHES * 128), BF16),
    pltpu.VMEM((OWN_ROWS, 128), F32),
    pltpu.VMEM((OWN_ROWS, 128), F32),
    pltpu.VMEM((PATCHES * 128 + 512, TILE), F32),
    pltpu.VMEM((PATCHES * 128 + 512, OWN_ROWS), BF16),
    pltpu.VMEM((PATCHES * 128, 512), F32),
    pltpu.VMEM((PATCHES * 128, 128), BF16),
]


def first_layer(received, frame_mod, maps):
    return pl.pallas_call(
        first_kernel,
        grid=(1,),
        in_specs=[
            pl.BlockSpec((1, PATCHES, CHUNK, 128), lambda i: (0, 0, 0, 0)),
            pl.BlockSpec((1, PATCHES, 64, 128), lambda i: (1, 0, 4, 0)),
            pl.BlockSpec((16, 384), lambda i: (0, 0)),
            pl.BlockSpec((3, 128), lambda i: (0, 0)),
        ],
        out_specs=[
            pl.BlockSpec((OWN_ROWS, 128), lambda i: (0, 0)),
            pl.BlockSpec((64, MID, 128), lambda i: (0, 0, 0)),
        ],
        out_shape=[
            jax.ShapeDtypeStruct((OWN_ROWS, 128), BF16),
            jax.ShapeDtypeStruct((64, MID, 128), BF16),
        ],
        scratch_shapes=SCRATCH + [pltpu.VMEM((OWN_ROWS, 128), F32)],
        compiler_params=PARAMS,
        name="first_layer",
    )(received, received, frame_mod, maps)


def second_kernel(scal, kv, own, after, before, sums, frame_mod, maps, x_out, qa, ka, vt, kf, vf, xo, go, sc, pt, mods, vh, rs):
    table = mod_table(frame_mod[...], False)
    gains = maps[...]
    third = scal[0]
    row = lax.broadcasted_iota(jnp.int32, (16, OWN_ROWS), 0)
    ones = jnp.where(lax.broadcasted_iota(jnp.int32, (16, 128), 0) < 3, 1.0, 0.0).astype(BF16)
    for k in range(3):
        which = lax.rem(third + k, 3)
        total = None
        for head in range(HEADS):
            at = 4 * head + which if head < 16 else 16 * (head - 16) + 4 * which + 3
            part = sums[at].astype(F32)
            total = part if total is None else total + part
        square = jnp.concatenate([total[8 + i : 9 + i] + total[18 + i : 19 + i] for i in range(10)], axis=1)
        hi, mid, low = split3(lax.rsqrt(square * (1.0 / WIDTH) + EPSILON))
        r = jnp.where(row == 0, hi, jnp.where(row == 1, mid, jnp.where(row == 2, low, 0.0)))
        rs[k] = dot(r.astype(BF16), ones, TN)

    modulations(kv, table, mods)
    for t in range(PATCHES // 2):
        at = slice(t * 80, t * 80 + 80)
        pair = [ref[at, :].astype(F32) for ref in (own, after, before)]
        scale = [rs[k, at, :] for k in range(3)]
        hids, gates = [], []
        for half in range(2):
            p = 2 * t + half
            cut = slice(THIRD * half, THIRD * half + THIRD)
            none = [jnp.zeros((8, 128), F32)]
            x = jnp.concatenate([v[cut] for v in pair] + none, axis=0)
            r = jnp.concatenate([v[cut] for v in scale] + none, axis=0)
            m = mods[p * 128 : p * 128 + 128, 0:384]
            hids.append(x * r * (1.0 + m[:, 128:256]) + m[:, 0:128])
            gates.append(m[0:THIRD, 256:384])
        place_pair(t, hids, gains, kv, qa, ka, vt, kf, vh)
        xo[at, :] = pair[0]
        go[at, :] = jnp.concatenate(gates, axis=0)
    turn_values(vh, vt, vf)

    def result(at, value):
        x_out[at, :] = value

    attention(qa, ka, vt, kf, vf, xo, go, sc, pt, result)


def second_layer(third, received, own, after, before, sums, frame_mod, maps):
    rows = pl.BlockSpec((OWN_ROWS, 128), lambda i, s: (0, 0))
    grid = pltpu.PrefetchScalarGridSpec(
        num_scalar_prefetch=1,
        grid=(1,),
        in_specs=[
            pl.BlockSpec((1, PATCHES, 256, 128), lambda i, s: (1, 0, 0, 0)),
            rows,
            rows,
            rows,
            pl.BlockSpec((64, 32, 128), lambda i, s: (0, 1, 0)),
            pl.BlockSpec((16, 384), lambda i, s: (0, 0)),
            pl.BlockSpec((3, 128), lambda i, s: (0, 0)),
        ],
        out_specs=rows,
        scratch_shapes=SCRATCH + [pltpu.VMEM((3, OWN_ROWS, 128), F32)],
    )
    return pl.pallas_call(
        second_kernel,
        grid_spec=grid,
        out_shape=jax.ShapeDtypeStruct((OWN_ROWS, 128), BF16),
        compiler_params=PARAMS,
        name="second_layer",
    )(third, received, own, after, before, sums, frame_mod, maps)


def home_kernel(scal, got, stream, frames, frame_mod, maps, out, xs, frame_row):
    section = scal[0]
    frame_row[0:1, 0:TOK] = frames[...].astype(F32)
    square = jnp.zeros((TOK, 128), F32)
    for head in range(HEADS):
        cols = slice(128 * head, 128 * head + 128)
        parts = [got[place_of(head, third)].astype(F32)[0:THIRD] for third in range(3)]
        x = jnp.where(section == 0, stream[:, cols].astype(F32), jnp.concatenate(parts, axis=0))
        xs[:, cols] = x
        square = square + x * x
    r = lax.rsqrt(jnp.sum(square, axis=1, keepdims=True) * (1.0 / WIDTH) + EPSILON)
    row = lax.broadcasted_iota(jnp.int32, (48, 128), 0)
    hot = jnp.where((row & 15).astype(F32) == frame_row[0:1, :], 1.0, 0.0).astype(BF16)
    for head in range(HEADS):
        cols = slice(128 * head, 128 * head + 128)
        more = slice(WIDTH + 128 * head, WIDTH + 128 * head + 128)
        mod = jnp.concatenate([frame_mod[:, cols], frame_mod[:, more]], axis=1)
        m = dot(hot, jnp.concatenate(split3(mod), axis=0).astype(BF16), TN)[0:TOK]
        hid = xs[:, cols] * r * (1.0 + m[:, 128:256]) + m[:, 0:128]
        out[0, :, cols] = (hid * maps[1:2, cols]).astype(BF16)
        out[1, :, cols] = (hid * maps[2:3, cols]).astype(BF16)


def home(section, got, stream, frames, frame_mod, maps):
    whole = pl.BlockSpec(memory_space=pltpu.VMEM)
    return pl.pallas_call(
        home_kernel,
        in_specs=[pl.BlockSpec(memory_space=pltpu.SMEM)] + [whole] * 5,
        out_specs=whole,
        out_shape=jax.ShapeDtypeStruct((2, TOK, WIDTH), BF16),
        scratch_shapes=[pltpu.VMEM((TOK, WIDTH), F32), pltpu.VMEM((8, 128), F32)],
        compiler_params=PARAMS,
        name="home",
    )(section, got, stream, frames, frame_mod, maps)


def mix_kernel(scal, mine, other, out):
    branch = scal[0]
    for t in range(PATCHES // 2):
        a = mine[80 * t : 80 * t + 80, :].astype(F32)
        b = other[80 * t : 80 * t + 80, :].astype(F32)
        cond, uncond = jnp.where(branch == 0, a, b), jnp.where(branch == 0, b, a)
        guided = uncond + GUIDE * (cond - uncond)
        for half in range(2):
            block = guided[THIRD * half : THIRD * half + THIRD].astype(BF16)
            out[2 * t + half] = block
            out[PATCHES + 2 * t + half] = block


def mix(branch, mine, other):
    whole = pl.BlockSpec(memory_space=pltpu.VMEM)
    return pl.pallas_call(
        mix_kernel,
        in_specs=[pl.BlockSpec(memory_space=pltpu.SMEM), whole, whole],
        out_specs=whole,
        out_shape=jax.ShapeDtypeStruct((64, THIRD, 128), BF16),
        compiler_params=PARAMS,
        name="mix",
    )(branch, mine, other)


def unpack_kernel(scal, got, out):
    branch = scal[0]
    for j in range(HEADS // 2):
        parts = []
        for third in range(3):
            a, b = place_of(j, third), place_of(j + HEADS // 2, third)
            parts.append(got[jnp.where(branch == 0, a, b)].astype(F32))
        out[:, 128 * j : 128 * j + 128] = jnp.concatenate(parts, axis=0).astype(BF16)


def unpack(branch, got):
    whole = pl.BlockSpec(memory_space=pltpu.VMEM)
    return pl.pallas_call(
        unpack_kernel,
        in_specs=[pl.BlockSpec(memory_space=pltpu.SMEM), whole],
        out_specs=whole,
        out_shape=jax.ShapeDtypeStruct((TOK, WIDTH // 2), BF16),
        compiler_params=PARAMS,
        name="unpack",
    )(branch, got)


def body(stream, token_frame, frame_levels, level_table, branch_mod, layer_mod, maps, stale_kv):
    section = lax.axis_index("section")
    branch = lax.axis_index("branch")
    place = section * PATCHES + lax.axis_index("patch")
    x, y, z = place % 4, (place // 4) % 4, place // 16
    head = jnp.where(x < 3, place // 4, 16 + z)
    third = jnp.where(x < 3, x, jnp.where(y < 3, y, 0))

    both = jnp.concatenate([layer_mod.reshape(3, WIDTH), maps[0]], axis=0)
    other = lax.ppermute(both, "section", [(0, 1), (1, 0)])

    frames = token_frame.reshape(1, TOK)
    section_at = section.reshape(1).astype(jnp.int32)
    send = pack(section_at, stale_kv[0, 0], stream, frames)
    received = lax.all_to_all(send, PLANE, 0, 0, tiled=True)
    received = received.reshape(2, PATCHES, CHUNK, 128)

    level_hot = (frame_levels[:, None] == jnp.arange(LEVELS, dtype=jnp.int32)[None, :]).astype(F32)
    base = jnp.dot(level_hot, level_table, precision=lax.Precision.HIGHEST, preferred_element_type=F32)
    home_mod = base + (layer_mod[0] + branch_mod[0])[None, :]

    def of_head(array):
        rows = array.shape[0]
        return lax.dynamic_slice_in_dim(array.reshape(rows, -1, HEADS, 128), head, 1, 2)[:, :, 0]

    layers = jnp.stack([jnp.where(section == 0, both, other), jnp.where(section == 0, other, both)])
    mine = of_head(layers.reshape(12, WIDTH)).reshape(2, 6, 128)
    base_mine = of_head(base)
    branch_mine = of_head(branch_mod)[0]
    mods = base_mine[None] + (mine[:, 0:3] + branch_mine[None])[:, None]
    mods = mods.reshape(2, FRAMES, 384)
    gains = mine[:, 3:6]

    x_one, mid = first_layer(received, mods[0], gains[0])

    def from_third(by):
        pairs = [(place_of(h, (g + by) % 3), place_of(h, g)) for h in range(HEADS) for g in range(3)]
        return lax.ppermute(x_one, PLANE, pairs)

    after, before = from_third(1), from_third(2)
    mid_got = lax.all_to_all(mid, PLANE, 0, 0, tiled=True)
    fresh = home(section_at, mid_got, stream, frames, home_mod, maps[0])
    x_two = second_layer(third.reshape(1).astype(jnp.int32), received, x_one, after, before, mid_got, mods[1], gains[1])

    x_other = lax.ppermute(x_two, "branch", [(0, 1), (1, 0)])
    branch_at = branch.reshape(1).astype(jnp.int32)
    guided = mix(branch_at, x_two, x_other)
    guided_got = lax.all_to_all(guided, PLANE, 0, 0, tiled=True)
    out = unpack(branch_at, guided_got)
    return (out, fresh[None, None])


def solution(mesh):
    placed = (
        P("patch", None),
        P("patch"),
        P(),
        P(),
        P("branch", None),
        P("section", None),
        P("section", None, None),
        P("branch", "section", None, "patch", None),
    )
    return jax.shard_map(
        body,
        mesh=mesh,
        in_specs=placed,
        out_specs=(P("patch", "branch"), P("branch", "section", None, "patch", None)),
        check_vma=False,
    )
```

profile of v0, /device:TPU:0, one launch (start us, length us, event | category | flops | bytes accessed | tf_op | source)
XLA Modules:
  0.0 205.1 jit_solution(2270458806535496251)
XLA Ops:
  0.6 0.0 copy-start
  0.7 4.9 %pack.1 = bf16[64,320,128]{2,1,0:T(8,128)(2,1)} custom-call(s32[1]{0:T(128)} %bitcast.2.scal, bf16[2,120,2560]{2,1,0:T(8,128)(2,1)} %bitcast.36, bf16[120,2560]{1,0:T(8,128)(2,1)} %stream.3, s32[1,120]{1,0:T(1,128)} %bitcast.46), custom_call_target="tpu_custom_call" | custom-call | tf_op jit(solution)/shard_map/pack/pallas_call | solution.py:129
  5.6 0.0 copy-start.9
  5.6 0.0 copy-start.7
  5.6 0.0 copy-start.8
  5.6 0.0 copy-start.10
  5.6 11.9 %all-to-all-start = ((bf16[64,320,128]{2,1,0:T(8,128)(2,1)}), bf16[64,320,128]{2,1,0:T(8,128)(2,1)}, u32[]{:S(2)}, u32[]{:S(2)}) async-start(bf16[64,320,128]{2,1,0:T(8,128)(2,1)} %pack.1), calls=%async_computation | async-start | bytes 10485760 | tf_op jit(solution)/shard_map/all_to_all | solution.py:534
  17.5 0.0 copy-done.9
  17.5 0.0 copy-done.7
  17.5 0.0 copy-done.8
  17.5 0.0 copy-start.3
  17.5 0.2 add_reduce_fusion
  17.8 3.2 %collective-permute-start = (f32[6,2560]{1,0:T(8,128)S(1)}, f32[6,2560]{1,0:T(8,128)S(1)}, u32[]{:S(2)}, u32[]{:S(2)}) collective-permute-start(f32[6,2560]{1,0:T(8,128)S(1)} %pad_maximum_fusion.1), channel_id=1, source_target_pairs={{0,32},{32,0},{1,33},{33,1},{2,34},{34,2},{3,35},{35,3},{4,36},{36... | collective-permute-start | bytes 184328 | tf_op jit(solution)/shard_map/ppermute | solution.py:529
  21.1 0.0 copy-done
  21.1 0.0 copy-done.10
  21.1 1.5 broadcast_add_fusion
  22.6 0.1 reshape.42
  22.7 12.8 %collective-permute-done = f32[6,2560]{1,0:T(8,128)S(1)} collective-permute-done((f32[6,2560]{1,0:T(8,128)S(1)}, f32[6,2560]{1,0:T(8,128)S(1)}, u32[]{:S(2)}, u32[]{:S(2)}) %collective-permute-start) | collective-permute-done | bytes 61472 | tf_op jit(solution)/shard_map/ppermute | solution.py:529
  35.5 0.0 copy-done.3
  35.7 0.6 copy.24
  36.3 0.6 slice_bitcast_fusion
  36.9 46.9 %all-to-all-done = bf16[64,320,128]{2,1,0:T(8,128)(2,1)} async-done(((bf16[64,320,128]{2,1,0:T(8,128)(2,1)}), bf16[64,320,128]{2,1,0:T(8,128)(2,1)}, u32[]{:S(2)}, u32[]{:S(2)}) %all-to-all-start) | async-done | bytes 5242912 | tf_op jit(solution)/shard_map/all_to_all | solution.py:534
  83.8 25.3 %first_layer.1 = (bf16[1280,128]{1,0:T(8,128)(2,1)}, bf16[64,64,128]{2,1,0:T(8,128)(2,1)}) custom-call(bf16[2,32,320,128]{3,2,1,0:T(8,128)(2,1)} %bitcast.5.kv.x_rest, bf16[2,32,320,128]{3,2,1,0:T(8,128)(2,1)} %bitcast.5.kv.x_rest, f32[16,384]{1,0:T(8,128)} %bitcast.43, f32[3,128]{1,0:T(4,128)} %get-tuple-element.14.maps), custom_call_target="tpu_custom_call" | custom-call | tf_op jit(solution)/shard_map/first_layer/pallas_call | solution.py:344
  109.1 0.0 copy-start.4
  109.1 11.4 %all-to-all-start.1 = ((bf16[64,64,128]{2,1,0:T(8,128)(2,1)}), bf16[64,64,128]{2,1,0:T(8,128)(2,1)S(1)}, u32[]{:S(2)}, u32[]{:S(2)}) async-start(bf16[64,64,128]{2,1,0:T(8,128)(2,1)} %get-tuple-element.5), calls=%async_computation.1 | async-start | bytes 2097152 | tf_op jit(solution)/shard_map/all_to_all | solution.py:560
  120.5 0.0 copy-done.4
  120.5 5.0 %collective-permute-start.1 = (bf16[1280,128]{1,0:T(8,128)(2,1)S(1)}, bf16[1280,128]{1,0:T(8,128)(2,1)S(1)}, u32[]{:S(2)}, u32[]{:S(2)}) collective-permute-start(bf16[1280,128]{1,0:T(8,128)(2,1)S(1)} %copy-done.4), channel_id=1, source_target_pairs={{1,0},{2,1},{0,2},{5,4},{6,5},{4,6},{9,8},{10,9},{8,10},{13,12},{1... | collective-permute-start | bytes 983048 | tf_op jit(solution)/shard_map/ppermute | solution.py:557
  125.5 1.9 collective-permute-start.2
  127.5 0.6 copy.23
  128.1 12.1 %collective-permute-done.1.after = bf16[1280,128]{1,0:T(8,128)(2,1)S(1)} collective-permute-done((bf16[1280,128]{1,0:T(8,128)(2,1)S(1)}, bf16[1280,128]{1,0:T(8,128)(2,1)S(1)}, u32[]{:S(2)}, u32[]{:S(2)}) %collective-permute-start.1) | collective-permute-done | bytes 327712 | tf_op jit(solution)/shard_map/ppermute | solution.py:557
  140.2 0.0 copy-start.5
  140.2 5.2 %collective-permute-done.2.before = bf16[1280,128]{1,0:T(8,128)(2,1)} collective-permute-done((bf16[1280,128]{1,0:T(8,128)(2,1)S(1)}, bf16[1280,128]{1,0:T(8,128)(2,1)}, u32[]{:S(2)}, u32[]{:S(2)}) %collective-permute-start.2) | collective-permute-done | bytes 327712 | tf_op jit(solution)/shard_map/ppermute | solution.py:557
  145.3 0.0 all-to-all-done.1.sums.got
  145.3 0.0 copy-start.1
  145.3 0.0 copy-done.5
  145.3 1.0 copy-done.1
  146.3 25.1 %second_layer.1.mine = bf16[1280,128]{1,0:T(8,128)(2,1)} custom-call(s32[1]{0:T(128)} %bitcast.1.scal, bf16[2,32,320,128]{3,2,1,0:T(8,128)(2,1)} %bitcast.5.kv.x_rest, bf16[1280,128]{1,0:T(8,128)(2,1)} %get-tuple-element.4.own, bf16[1280,128]{1,0:T(8,128)(2,1)} %copy-done.5, bf16[1280,128]{1,0:T(8,128)(2,1)} %collective-permute-done.2.before, ...), custom_call_target="tpu_custom_call" | custom-call | tf_op jit(solution)/shard_map/second_layer/pallas_call | solution.py:428
  171.4 0.0 collective-permute-start.3
  171.4 1.8 collective-permute-done.3.other
  173.3 0.0 copy-start.6
  173.3 0.7 copy-done.6
  174.0 2.1 %mix.1 = bf16[64,40,128]{2,1,0:T(8,128)(2,1)} custom-call(s32[1]{0:T(128)} %bitcast.scal, bf16[1280,128]{1,0:T(8,128)(2,1)} %second_layer.1.mine, bf16[1280,128]{1,0:T(8,128)(2,1)} %copy-done.6), custom_call_target="tpu_custom_call" | custom-call | tf_op jit(solution)/shard_map/mix/pallas_call | solution.py:488
  176.1 11.3 %all-to-all-start.2 = ((bf16[64,40,128]{2,1,0:T(8,128)(2,1)}), bf16[64,40,128]{2,1,0:T(8,128)(2,1)S(1)}, u32[]{:S(2)}, u32[]{:S(2)}) async-start(bf16[64,40,128]{2,1,0:T(8,128)(2,1)} %mix.1), calls=%async_computation.2 | async-start | bytes 1310720 | tf_op jit(solution)/shard_map/all_to_all | solution.py:567
  187.4 3.3 %home.1 = bf16[2,120,2560]{2,1,0:T(8,128)(2,1)} custom-call(s32[1]{0:T(128)} %bitcast.2.scal, bf16[64,64,128]{2,1,0:T(8,128)(2,1)} %copy-done.1, bf16[120,2560]{1,0:T(8,128)(2,1)} %stream.3, s32[1,120]{1,0:T(1,128)} %bitcast.47, f32[16,7680]{1,0:T(8,128)} %get-tuple-element.15.frame_mod, f32[3,2560]{1,0:T(4,128)} %bitcast.39), custom_call_target="tpu_custom_call" | custom-call | tf_op jit(solution)/shard_map/home/pallas_call | solution.py:462
  190.6 11.8 %all-to-all-done.2.got = bf16[64,40,128]{2,1,0:T(8,128)(2,1)S(1)} async-done(((bf16[64,40,128]{2,1,0:T(8,128)(2,1)}), bf16[64,40,128]{2,1,0:T(8,128)(2,1)S(1)}, u32[]{:S(2)}, u32[]{:S(2)}) %all-to-all-start.2) | async-done | bytes 655392 | tf_op jit(solution)/shard_map/all_to_all | solution.py:567
  202.4 0.0 copy-start.2
  202.4 0.8 copy-done.2
  203.3 1.9 unpack.1
  (17 shorter events, 0.3 us)
Async XLA Ops:
  0.6 20.4 %copy-start = (f32[50,7680]{1,0:T(8,128)S(1)}, f32[50,7680]{1,0:T(8,128)}, u32[]{:S(2)}) copy-start(f32[50,7680]{1,0:T(8,128)} %param.11) | copy-start | bytes 4608004
  5.6 11.9 %copy-start.9 = (f32[1,3,2560]{2,0,1:T(1,128)S(1)}, f32[1,3,2560]{2,0,1:T(1,128)}, u32[]{:S(2)}) copy-start(f32[1,3,2560]{2,0,1:T(1,128)} %param.14) | copy-start | bytes 92164
  5.6 11.9 %copy-start.7 = (f32[1,7680]{1,0:T(1,128)S(1)}, f32[1,7680]{1,0:T(1,128)}, u32[]{:S(2)}) copy-start(f32[1,7680]{1,0:T(1,128)} %param.13) | copy-start | bytes 92164
  5.6 11.9 %copy-start.8 = (f32[1,7680]{1,0:T(1,128)S(1)}, f32[1,7680]{1,0:T(1,128)}, u32[]{:S(2)}) copy-start(f32[1,7680]{1,0:T(1,128)} %param.12) | copy-start | bytes 92164
  5.6 15.5 %copy-start.10 = (s32[16]{0:T(128)S(1)}, s32[16]{0:T(128)}, u32[]{:S(2)}) copy-start(s32[16]{0:T(128)} %param.10) | copy-start | bytes 196
  5.6 78.2 %all-to-all-start = ((bf16[64,320,128]{2,1,0:T(8,128)(2,1)}), bf16[64,320,128]{2,1,0:T(8,128)(2,1)}, u32[]{:S(2)}, u32[]{:S(2)}) async-start(bf16[64,320,128]{2,1,0:T(8,128)(2,1)} %pack.1), calls=%async_computation | async-start | bytes 10485760 | tf_op jit(solution)/shard_map/all_to_all | solution.py:534
  17.5 18.0 %copy-start.3 = (f32[1,3,2560]{2,1,0:T(4,128)}, f32[1,3,2560]{2,1,0:T(4,128)S(1)}, u32[]{:S(2)}) copy-start(f32[1,3,2560]{2,1,0:T(4,128)S(1)} %copy.22) | copy-start | bytes 92164
  17.8 17.6 %collective-permute-start = (f32[6,2560]{1,0:T(8,128)S(1)}, f32[6,2560]{1,0:T(8,128)S(1)}, u32[]{:S(2)}, u32[]{:S(2)}) collective-permute-start(f32[6,2560]{1,0:T(8,128)S(1)} %pad_maximum_fusion.1), channel_id=1, source_target_pairs={{0,32},{32,0},{1,33},{33,1},{2,34},{34,2},{3,35},{35,3},{4,36},{36... | collective-permute-start | bytes 184328 | tf_op jit(solution)/shard_map/ppermute | solution.py:529
  109.1 11.4 %copy-start.4 = (bf16[1280,128]{1,0:T(8,128)(2,1)S(1)}, bf16[1280,128]{1,0:T(8,128)(2,1)}, u32[]{:S(2)}) copy-start(bf16[1280,128]{1,0:T(8,128)(2,1)} %get-tuple-element.4.own) | copy-start | bytes 983044
  109.1 36.2 %all-to-all-start.1 = ((bf16[64,64,128]{2,1,0:T(8,128)(2,1)}), bf16[64,64,128]{2,1,0:T(8,128)(2,1)S(1)}, u32[]{:S(2)}, u32[]{:S(2)}) async-start(bf16[64,64,128]{2,1,0:T(8,128)(2,1)} %get-tuple-element.5), calls=%async_computation.1 | async-start | bytes 2097152 | tf_op jit(solution)/shard_map/all_to_all | solution.py:560
  120.5 19.6 %collective-permute-start.1 = (bf16[1280,128]{1,0:T(8,128)(2,1)S(1)}, bf16[1280,128]{1,0:T(8,128)(2,1)S(1)}, u32[]{:S(2)}, u32[]{:S(2)}) collective-permute-start(bf16[1280,128]{1,0:T(8,128)(2,1)S(1)} %copy-done.4), channel_id=1, source_target_pairs={{1,0},{2,1},{0,2},{5,4},{6,5},{4,6},{9,8},{10,9},{8,10},{13,12},{1... | collective-permute-start | bytes 983048 | tf_op jit(solution)/shard_map/ppermute | solution.py:557
  125.5 19.8 %collective-permute-start.2 = (bf16[1280,128]{1,0:T(8,128)(2,1)S(1)}, bf16[1280,128]{1,0:T(8,128)(2,1)}, u32[]{:S(2)}, u32[]{:S(2)}) collective-permute-start(bf16[1280,128]{1,0:T(8,128)(2,1)S(1)} %copy-done.4), channel_id=1, source_target_pairs={{2,0},{0,1},{1,2},{6,4},{4,5},{5,6},{10,8},{8,9},{9,10},{14,12},{1... | collective-permute-start | bytes 983048 | tf_op jit(solution)/shard_map/ppermute | solution.py:557
  140.2 5.2 %copy-start.5 = (bf16[1280,128]{1,0:T(8,128)(2,1)}, bf16[1280,128]{1,0:T(8,128)(2,1)S(1)}, u32[]{:S(2)}) copy-start(bf16[1280,128]{1,0:T(8,128)(2,1)S(1)} %collective-permute-done.1.after) | copy-start | bytes 983044
  145.3 1.0 copy-start.1
  171.4 1.8 collective-permute-start.3
  173.3 0.7 copy-start.6
  176.1 26.3 %all-to-all-start.2 = ((bf16[64,40,128]{2,1,0:T(8,128)(2,1)}), bf16[64,40,128]{2,1,0:T(8,128)(2,1)S(1)}, u32[]{:S(2)}, u32[]{:S(2)}) async-start(bf16[64,40,128]{2,1,0:T(8,128)(2,1)} %mix.1), calls=%async_computation.2 | async-start | bytes 1310720 | tf_op jit(solution)/shard_map/all_to_all | solution.py:567
  202.4 0.8 copy-start.2
where the time goes:
time: 206 us; the launch traced here: 205 us
  waiting for transfers between devices  90.5 us (44%)
  Pallas kernels  62.6 us (30%)
  starting transfers between devices  44.7 us (22%)
  local copies, waits for them, and re-layouts  4.66 us (2%)
    all_to_all x1, waiting for transfers between devices, body(): received = lax.all_to_all(send, PLANE, 0, 0, tiled=True)  46.9 us
    pallas_call x1, Pallas kernels, first_layer(): pl.pallas_call(first_kernel, grid=(1,), in_specs=[pl.BlockSpec((1, PATCHE...  25.3 us
    pallas_call x1, Pallas kernels, second_layer(): pl.pallas_call(second_kernel, grid_spec=grid, out_shape=jax.ShapeDtypeStr...  25.1 us
    ppermute x2, waiting for transfers between devices, from_third(): return lax.ppermute(x_one, PLANE, pairs)  17.2 us
    ppermute x1, waiting for transfers between devices, body(): other = lax.ppermute(both, 'section', [(0, 1), (1, 0)])  12.8 us
    all_to_all x1, starting transfers between devices, body(): received = lax.all_to_all(send, PLANE, 0, 0, tiled=True)  11.9 us
    all_to_all x1, waiting for transfers between devices, body(): guided_got = lax.all_to_all(guided, PLANE, 0, 0, tiled=True)  11.8 us
    all_to_all x1, starting transfers between devices, body(): mid_got = lax.all_to_all(mid, PLANE, 0, 0, tiled=True)  11.4 us
  transfers between devices with their start and end apart: 7, of which 6 were waited for; matrix products, arithmetic and copies ran while one was open for 2% of the time, Pallas kernels for 2%

commit v1 on v0

--- a/solution.py
+++ b/solution.py
@@ -42,6 +42,10 @@
 
 def dot(a, b, dims):
     return lax.dot_general(a, b, (dims, ((), ())), preferred_element_type=F32)
+
+
+def block(shape):
+    return pl.BlockSpec(shape, lambda i: (0,) * len(shape))
 
 
 NN = ((1,), (0,))
@@ -458,11 +462,12 @@
 
 
 def home(section, got, stream, frames, frame_mod, maps):
-    whole = pl.BlockSpec(memory_space=pltpu.VMEM)
+    operands = [got, stream, frames, frame_mod, maps]
     return pl.pallas_call(
         home_kernel,
-        in_specs=[pl.BlockSpec(memory_space=pltpu.SMEM)] + [whole] * 5,
-        out_specs=whole,
+        grid=(1,),
+        in_specs=[pl.BlockSpec(memory_space=pltpu.SMEM)] + [block(v.shape) for v in operands],
+        out_specs=block((2, TOK, WIDTH)),
         out_shape=jax.ShapeDtypeStruct((2, TOK, WIDTH), BF16),
         scratch_shapes=[pltpu.VMEM((TOK, WIDTH), F32), pltpu.VMEM((8, 128), F32)],
         compiler_params=PARAMS,
@@ -484,11 +489,11 @@
 
 
 def mix(branch, mine, other):
-    whole = pl.BlockSpec(memory_space=pltpu.VMEM)
     return pl.pallas_call(
         mix_kernel,
-        in_specs=[pl.BlockSpec(memory_space=pltpu.SMEM), whole, whole],
-        out_specs=whole,
+        grid=(1,),
+        in_specs=[pl.BlockSpec(memory_space=pltpu.SMEM), block(mine.shape), block(other.shape)],
+        out_specs=block((64, THIRD, 128)),
         out_shape=jax.ShapeDtypeStruct((64, THIRD, 128), BF16),
         compiler_params=PARAMS,
         name="mix",
@@ -506,11 +511,11 @@
 
 
 def unpack(branch, got):
-    whole = pl.BlockSpec(memory_space=pltpu.VMEM)
     return pl.pallas_call(
         unpack_kernel,
-        in_specs=[pl.BlockSpec(memory_space=pltpu.SMEM), whole],
-        out_specs=whole,
+        grid=(1,),
+        in_specs=[pl.BlockSpec(memory_space=pltpu.SMEM), block(got.shape)],
+        out_specs=block((TOK, WIDTH // 2)),
         out_shape=jax.ShapeDtypeStruct((TOK, WIDTH // 2), BF16),
         compiler_params=PARAMS,
         name="unpack",

time: 206 us -> 206 us (level)
  no operation moved by 1% of the time
where the time goes in v1:
time: 206 us; the launch traced here: 205 us
  waiting for transfers between devices  90.5 us (44%)
  Pallas kernels  62.6 us (30%)
  starting transfers between devices  44.7 us (22%)
  local copies, waits for them, and re-layouts  4.66 us (2%)
    all_to_all x1, waiting for transfers between devices, body(): received = lax.all_to_all(send, PLANE, 0, 0, tiled=True)  46.9 us
    pallas_call x1, Pallas kernels, first_layer(): pl.pallas_call(first_kernel, grid=(1,), in_specs=[pl.BlockSpec((1, PATCHE...  25.3 us
    pallas_call x1, Pallas kernels, second_layer(): pl.pallas_call(second_kernel, grid_spec=grid, out_shape=jax.ShapeDtypeStr...  25.1 us
    ppermute x2, waiting for transfers between devices, from_third(): return lax.ppermute(x_one, PLANE, pairs)  17.2 us
    ppermute x1, waiting for transfers between devices, body(): other = lax.ppermute(both, 'section', [(0, 1), (1, 0)])  12.8 us
    all_to_all x1, starting transfers between devices, body(): received = lax.all_to_all(send, PLANE, 0, 0, tiled=True)  11.9 us
    all_to_all x1, waiting for transfers between devices, body(): guided_got = lax.all_to_all(guided, PLANE, 0, 0, tiled=True)  11.8 us
    all_to_all x1, starting transfers between devices, body(): mid_got = lax.all_to_all(mid, PLANE, 0, 0, tiled=True)  11.4 us
  transfers between devices with their start and end apart: 7, of which 6 were waited for; matrix products, arithmetic and copies ran while one was open for 2% of the time, Pallas kernels for 2%

profile of v1, /device:TPU:0, one launch (start us, length us, event | category | flops | bytes accessed | tf_op | source)
XLA Modules:
  0.0 205.1 jit_solution(2270458806535496251)
XLA Ops:
  0.6 0.0 copy-start
  0.7 4.9 %pack.1 = bf16[64,320,128]{2,1,0:T(8,128)(2,1)} custom-call(s32[1]{0:T(128)} %bitcast.2.scal, bf16[2,120,2560]{2,1,0:T(8,128)(2,1)} %bitcast.36, bf16[120,2560]{1,0:T(8,128)(2,1)} %stream.3, s32[1,120]{1,0:T(1,128)} %bitcast.46), custom_call_target="tpu_custom_call" | custom-call | tf_op jit(solution)/shard_map/pack/pallas_call | solution.py:133
  5.6 0.0 copy-start.9
  5.6 0.0 copy-start.7
  5.6 0.0 copy-start.8
  5.6 0.0 copy-start.10
  5.6 11.9 %all-to-all-start = ((bf16[64,320,128]{2,1,0:T(8,128)(2,1)}), bf16[64,320,128]{2,1,0:T(8,128)(2,1)}, u32[]{:S(2)}, u32[]{:S(2)}) async-start(bf16[64,320,128]{2,1,0:T(8,128)(2,1)} %pack.1), calls=%async_computation | async-start | bytes 10485760 | tf_op jit(solution)/shard_map/all_to_all | solution.py:539
  17.5 0.0 copy-done.9
  17.5 0.0 copy-done.7
  17.5 0.0 copy-done.8
  17.5 0.0 copy-start.3
  17.5 0.2 add_reduce_fusion
  17.8 3.2 %collective-permute-start = (f32[6,2560]{1,0:T(8,128)S(1)}, f32[6,2560]{1,0:T(8,128)S(1)}, u32[]{:S(2)}, u32[]{:S(2)}) collective-permute-start(f32[6,2560]{1,0:T(8,128)S(1)} %pad_maximum_fusion.1), channel_id=1, source_target_pairs={{0,32},{32,0},{1,33},{33,1},{2,34},{34,2},{3,35},{35,3},{4,36},{36... | collective-permute-start | bytes 184328 | tf_op jit(solution)/shard_map/ppermute | solution.py:534
  21.1 0.0 copy-done
  21.1 0.0 copy-done.10
  21.1 1.5 broadcast_add_fusion
  22.6 0.1 reshape.42
  22.7 12.8 %collective-permute-done = f32[6,2560]{1,0:T(8,128)S(1)} collective-permute-done((f32[6,2560]{1,0:T(8,128)S(1)}, f32[6,2560]{1,0:T(8,128)S(1)}, u32[]{:S(2)}, u32[]{:S(2)}) %collective-permute-start) | collective-permute-done | bytes 61472 | tf_op jit(solution)/shard_map/ppermute | solution.py:534
  35.5 0.0 copy-done.3
  35.7 0.6 copy.24
  36.3 0.6 slice_bitcast_fusion
  36.9 46.9 %all-to-all-done = bf16[64,320,128]{2,1,0:T(8,128)(2,1)} async-done(((bf16[64,320,128]{2,1,0:T(8,128)(2,1)}), bf16[64,320,128]{2,1,0:T(8,128)(2,1)}, u32[]{:S(2)}, u32[]{:S(2)}) %all-to-all-start) | async-done | bytes 5242912 | tf_op jit(solution)/shard_map/all_to_all | solution.py:539
  83.8 25.3 %first_layer.1 = (bf16[1280,128]{1,0:T(8,128)(2,1)}, bf16[64,64,128]{2,1,0:T(8,128)(2,1)}) custom-call(bf16[2,32,320,128]{3,2,1,0:T(8,128)(2,1)} %bitcast.5.kv.x_rest, bf16[2,32,320,128]{3,2,1,0:T(8,128)(2,1)} %bitcast.5.kv.x_rest, f32[16,384]{1,0:T(8,128)} %bitcast.43, f32[3,128]{1,0:T(4,128)} %get-tuple-element.14.maps), custom_call_target="tpu_custom_call" | custom-call | tf_op jit(solution)/shard_map/first_layer/pallas_call | solution.py:348
  109.1 0.0 copy-start.4
  109.1 11.4 %all-to-all-start.1 = ((bf16[64,64,128]{2,1,0:T(8,128)(2,1)}), bf16[64,64,128]{2,1,0:T(8,128)(2,1)S(1)}, u32[]{:S(2)}, u32[]{:S(2)}) async-start(bf16[64,64,128]{2,1,0:T(8,128)(2,1)} %get-tuple-element.5), calls=%async_computation.1 | async-start | bytes 2097152 | tf_op jit(solution)/shard_map/all_to_all | solution.py:565
  120.5 0.0 copy-done.4
  120.5 5.0 %collective-permute-start.1 = (bf16[1280,128]{1,0:T(8,128)(2,1)S(1)}, bf16[1280,128]{1,0:T(8,128)(2,1)S(1)}, u32[]{:S(2)}, u32[]{:S(2)}) collective-permute-start(bf16[1280,128]{1,0:T(8,128)(2,1)S(1)} %copy-done.4), channel_id=1, source_target_pairs={{1,0},{2,1},{0,2},{5,4},{6,5},{4,6},{9,8},{10,9},{8,10},{13,12},{1... | collective-permute-start | bytes 983048 | tf_op jit(solution)/shard_map/ppermute | solution.py:562
  125.5 1.9 collective-permute-start.2
  127.5 0.6 copy.23
  128.1 12.1 %collective-permute-done.1.after = bf16[1280,128]{1,0:T(8,128)(2,1)S(1)} collective-permute-done((bf16[1280,128]{1,0:T(8,128)(2,1)S(1)}, bf16[1280,128]{1,0:T(8,128)(2,1)S(1)}, u32[]{:S(2)}, u32[]{:S(2)}) %collective-permute-start.1) | collective-permute-done | bytes 327712 | tf_op jit(solution)/shard_map/ppermute | solution.py:562
  140.2 0.0 copy-start.5
  140.2 5.2 %collective-permute-done.2.before = bf16[1280,128]{1,0:T(8,128)(2,1)} collective-permute-done((bf16[1280,128]{1,0:T(8,128)(2,1)S(1)}, bf16[1280,128]{1,0:T(8,128)(2,1)}, u32[]{:S(2)}, u32[]{:S(2)}) %collective-permute-start.2) | collective-permute-done | bytes 327712 | tf_op jit(solution)/shard_map/ppermute | solution.py:562
  145.3 0.0 all-to-all-done.1.sums.got
  145.3 0.0 copy-start.1
  145.3 0.0 copy-done.5
  145.3 1.0 copy-done.1
  146.3 25.1 %second_layer.1.mine = bf16[1280,128]{1,0:T(8,128)(2,1)} custom-call(s32[1]{0:T(128)} %bitcast.1.scal, bf16[2,32,320,128]{3,2,1,0:T(8,128)(2,1)} %bitcast.5.kv.x_rest, bf16[1280,128]{1,0:T(8,128)(2,1)} %get-tuple-element.4.own, bf16[1280,128]{1,0:T(8,128)(2,1)} %copy-done.5, bf16[1280,128]{1,0:T(8,128)(2,1)} %collective-permute-done.2.before, ...), custom_call_target="tpu_custom_call" | custom-call | tf_op jit(solution)/shard_map/second_layer/pallas_call | solution.py:432
  171.4 0.0 collective-permute-start.3
  171.4 1.8 collective-permute-done.3.other
  173.3 0.0 copy-start.6
  173.3 0.7 copy-done.6
  174.0 2.1 %mix.1 = bf16[64,40,128]{2,1,0:T(8,128)(2,1)} custom-call(s32[1]{0:T(128)} %bitcast.scal, bf16[1280,128]{1,0:T(8,128)(2,1)} %second_layer.1.mine, bf16[1280,128]{1,0:T(8,128)(2,1)} %copy-done.6), custom_call_target="tpu_custom_call" | custom-call | tf_op jit(solution)/shard_map/mix/pallas_call | solution.py:492
  176.1 11.3 %all-to-all-start.2 = ((bf16[64,40,128]{2,1,0:T(8,128)(2,1)}), bf16[64,40,128]{2,1,0:T(8,128)(2,1)S(1)}, u32[]{:S(2)}, u32[]{:S(2)}) async-start(bf16[64,40,128]{2,1,0:T(8,128)(2,1)} %mix.1), calls=%async_computation.2 | async-start | bytes 1310720 | tf_op jit(solution)/shard_map/all_to_all | solution.py:572
  187.4 3.3 %home.1 = bf16[2,120,2560]{2,1,0:T(8,128)(2,1)} custom-call(s32[1]{0:T(128)} %bitcast.2.scal, bf16[64,64,128]{2,1,0:T(8,128)(2,1)} %copy-done.1, bf16[120,2560]{1,0:T(8,128)(2,1)} %stream.3, s32[1,120]{1,0:T(1,128)} %bitcast.47, f32[16,7680]{1,0:T(8,128)} %get-tuple-element.15.frame_mod, f32[3,2560]{1,0:T(4,128)} %bitcast.39), custom_call_target="tpu_custom_call" | custom-call | tf_op jit(solution)/shard_map/home/pallas_call | solution.py:466
  190.6 11.8 %all-to-all-done.2.got = bf16[64,40,128]{2,1,0:T(8,128)(2,1)S(1)} async-done(((bf16[64,40,128]{2,1,0:T(8,128)(2,1)}), bf16[64,40,128]{2,1,0:T(8,128)(2,1)S(1)}, u32[]{:S(2)}, u32[]{:S(2)}) %all-to-all-start.2) | async-done | bytes 655392 | tf_op jit(solution)/shard_map/all_to_all | solution.py:572
  202.4 0.0 copy-start.2
  202.4 0.8 copy-done.2
  203.3 1.9 unpack.1
  (17 shorter events, 0.3 us)
Async XLA Ops:
  0.6 20.4 %copy-start = (f32[50,7680]{1,0:T(8,128)S(1)}, f32[50,7680]{1,0:T(8,128)}, u32[]{:S(2)}) copy-start(f32[50,7680]{1,0:T(8,128)} %param.11) | copy-start | bytes 4608004
  5.6 11.9 %copy-start.9 = (f32[1,3,2560]{2,0,1:T(1,128)S(1)}, f32[1,3,2560]{2,0,1:T(1,128)}, u32[]{:S(2)}) copy-start(f32[1,3,2560]{2,0,1:T(1,128)} %param.14) | copy-start | bytes 92164
  5.6 11.9 %copy-start.7 = (f32[1,7680]{1,0:T(1,128)S(1)}, f32[1,7680]{1,0:T(1,128)}, u32[]{:S(2)}) copy-start(f32[1,7680]{1,0:T(1,128)} %param.13) | copy-start | bytes 92164
  5.6 11.9 %copy-start.8 = (f32[1,7680]{1,0:T(1,128)S(1)}, f32[1,7680]{1,0:T(1,128)}, u32[]{:S(2)}) copy-start(f32[1,7680]{1,0:T(1,128)} %param.12) | copy-start | bytes 92164
  5.6 15.5 %copy-start.10 = (s32[16]{0:T(128)S(1)}, s32[16]{0:T(128)}, u32[]{:S(2)}) copy-start(s32[16]{0:T(128)} %param.10) | copy-start | bytes 196
  5.6 78.2 %all-to-all-start = ((bf16[64,320,128]{2,1,0:T(8,128)(2,1)}), bf16[64,320,128]{2,1,0:T(8,128)(2,1)}, u32[]{:S(2)}, u32[]{:S(2)}) async-start(bf16[64,320,128]{2,1,0:T(8,128)(2,1)} %pack.1), calls=%async_computation | async-start | bytes 10485760 | tf_op jit(solution)/shard_map/all_to_all | solution.py:539
  17.5 18.0 %copy-start.3 = (f32[1,3,2560]{2,1,0:T(4,128)}, f32[1,3,2560]{2,1,0:T(4,128)S(1)}, u32[]{:S(2)}) copy-start(f32[1,3,2560]{2,1,0:T(4,128)S(1)} %copy.22) | copy-start | bytes 92164
  17.8 17.6 %collective-permute-start = (f32[6,2560]{1,0:T(8,128)S(1)}, f32[6,2560]{1,0:T(8,128)S(1)}, u32[]{:S(2)}, u32[]{:S(2)}) collective-permute-start(f32[6,2560]{1,0:T(8,128)S(1)} %pad_maximum_fusion.1), channel_id=1, source_target_pairs={{0,32},{32,0},{1,33},{33,1},{2,34},{34,2},{3,35},{35,3},{4,36},{36... | collective-permute-start | bytes 184328 | tf_op jit(solution)/shard_map/ppermute | solution.py:534
  109.1 11.4 %copy-start.4 = (bf16[1280,128]{1,0:T(8,128)(2,1)S(1)}, bf16[1280,128]{1,0:T(8,128)(2,1)}, u32[]{:S(2)}) copy-start(bf16[1280,128]{1,0:T(8,128)(2,1)} %get-tuple-element.4.own) | copy-start | bytes 983044
  109.1 36.2 %all-to-all-start.1 = ((bf16[64,64,128]{2,1,0:T(8,128)(2,1)}), bf16[64,64,128]{2,1,0:T(8,128)(2,1)S(1)}, u32[]{:S(2)}, u32[]{:S(2)}) async-start(bf16[64,64,128]{2,1,0:T(8,128)(2,1)} %get-tuple-element.5), calls=%async_computation.1 | async-start | bytes 2097152 | tf_op jit(solution)/shard_map/all_to_all | solution.py:565
  120.5 19.6 %collective-permute-start.1 = (bf16[1280,128]{1,0:T(8,128)(2,1)S(1)}, bf16[1280,128]{1,0:T(8,128)(2,1)S(1)}, u32[]{:S(2)}, u32[]{:S(2)}) collective-permute-start(bf16[1280,128]{1,0:T(8,128)(2,1)S(1)} %copy-done.4), channel_id=1, source_target_pairs={{1,0},{2,1},{0,2},{5,4},{6,5},{4,6},{9,8},{10,9},{8,10},{13,12},{1... | collective-permute-start | bytes 983048 | tf_op jit(solution)/shard_map/ppermute | solution.py:562
  125.5 19.8 %collective-permute-start.2 = (bf16[1280,128]{1,0:T(8,128)(2,1)S(1)}, bf16[1280,128]{1,0:T(8,128)(2,1)}, u32[]{:S(2)}, u32[]{:S(2)}) collective-permute-start(bf16[1280,128]{1,0:T(8,128)(2,1)S(1)} %copy-done.4), channel_id=1, source_target_pairs={{2,0},{0,1},{1,2},{6,4},{4,5},{5,6},{10,8},{8,9},{9,10},{14,12},{1... | collective-permute-start | bytes 983048 | tf_op jit(solution)/shard_map/ppermute | solution.py:562
  140.2 5.2 %copy-start.5 = (bf16[1280,128]{1,0:T(8,128)(2,1)}, bf16[1280,128]{1,0:T(8,128)(2,1)S(1)}, u32[]{:S(2)}) copy-start(bf16[1280,128]{1,0:T(8,128)(2,1)S(1)} %collective-permute-done.1.after) | copy-start | bytes 983044
  145.3 1.0 copy-start.1
  171.4 1.8 collective-permute-start.3
  173.3 0.7 copy-start.6
  176.1 26.3 %all-to-all-start.2 = ((bf16[64,40,128]{2,1,0:T(8,128)(2,1)}), bf16[64,40,128]{2,1,0:T(8,128)(2,1)S(1)}, u32[]{:S(2)}, u32[]{:S(2)}) async-start(bf16[64,40,128]{2,1,0:T(8,128)(2,1)} %mix.1), calls=%async_computation.2 | async-start | bytes 1310720 | tf_op jit(solution)/shard_map/all_to_all | solution.py:572
  202.4 0.8 copy-start.2

commit v2 on v1

--- a/solution.py
+++ b/solution.py
@@ -477,24 +477,25 @@
 
 def mix_kernel(scal, mine, other, out):
     branch = scal[0]
-    for t in range(PATCHES // 2):
+    for t in range(4):
         a = mine[80 * t : 80 * t + 80, :].astype(F32)
         b = other[80 * t : 80 * t + 80, :].astype(F32)
         cond, uncond = jnp.where(branch == 0, a, b), jnp.where(branch == 0, b, a)
         guided = uncond + GUIDE * (cond - uncond)
         for half in range(2):
             block = guided[THIRD * half : THIRD * half + THIRD].astype(BF16)
-            out[2 * t + half] = block
-            out[PATCHES + 2 * t + half] = block
+            out[0, 2 * t + half] = block
+            out[1, 2 * t + half] = block
 
 
 def mix(branch, mine, other):
+    rows = pl.BlockSpec((8 * THIRD, 128), lambda i: (i, 0))
     return pl.pallas_call(
         mix_kernel,
-        grid=(1,),
-        in_specs=[pl.BlockSpec(memory_space=pltpu.SMEM), block(mine.shape), block(other.shape)],
-        out_specs=block((64, THIRD, 128)),
-        out_shape=jax.ShapeDtypeStruct((64, THIRD, 128), BF16),
+        grid=(PATCHES // 8,),
+        in_specs=[pl.BlockSpec(memory_space=pltpu.SMEM), rows, rows],
+        out_specs=pl.BlockSpec((2, 8, THIRD, 128), lambda i: (0, i, 0, 0)),
+        out_shape=jax.ShapeDtypeStruct((2, PATCHES, THIRD, 128), BF16),
         compiler_params=PARAMS,
         name="mix",
     )(branch, mine, other)
@@ -568,7 +569,7 @@
 
     x_other = lax.ppermute(x_two, "branch", [(0, 1), (1, 0)])
     branch_at = branch.reshape(1).astype(jnp.int32)
-    guided = mix(branch_at, x_two, x_other)
+    guided = mix(branch_at, x_two, x_other).reshape(64, THIRD, 128)
     guided_got = lax.all_to_all(guided, PLANE, 0, 0, tiled=True)
     out = unpack(branch_at, guided_got)
     return (out, fresh[None, None])

time: 206 us -> 207 us (level)
  no operation moved by 1% of the time
where the time goes in v2:
time: 207 us; the launch traced here: 206 us
  waiting for transfers between devices  90.5 us (44%)
  Pallas kernels  63.8 us (31%)
  starting transfers between devices  44.7 us (22%)
  local copies, waits for them, and re-layouts  4.66 us (2%)
    all_to_all x1, waiting for transfers between devices, body(): received = lax.all_to_all(send, PLANE, 0, 0, tiled=True)  46.9 us
    pallas_call x1, Pallas kernels, first_layer(): pl.pallas_call(first_kernel, grid=(1,), in_specs=[pl.BlockSpec((1, PATCHE...  25.3 us
    pallas_call x1, Pallas kernels, second_layer(): pl.pallas_call(second_kernel, grid_spec=grid, out_shape=jax.ShapeDtypeStr...  25.1 us
    ppermute x2, waiting for transfers between devices, from_third(): return lax.ppermute(x_one, PLANE, pairs)  17.2 us
    ppermute x1, waiting for transfers between devices, body(): other = lax.ppermute(both, 'section', [(0, 1), (1, 0)])  12.8 us
    all_to_all x1, starting transfers between devices, body(): received = lax.all_to_all(send, PLANE, 0, 0, tiled=True)  11.9 us
    all_to_all x1, waiting for transfers between devices, body(): guided_got = lax.all_to_all(guided, PLANE, 0, 0, tiled=True)  11.8 us
    all_to_all x1, starting transfers between devices, body(): mid_got = lax.all_to_all(mid, PLANE, 0, 0, tiled=True)  11.4 us
  transfers between devices with their start and end apart: 7, of which 6 were waited for; matrix products, arithmetic and copies ran while one was open for 2% of the time, Pallas kernels for 2%

profile of v2, /device:TPU:0, one launch (start us, length us, event | category | flops | bytes accessed | tf_op | source)
XLA Modules:
  0.0 206.4 jit_solution(14845287467250730800)
XLA Ops:
  0.6 0.0 copy-start
  0.7 4.9 %pack.1 = bf16[64,320,128]{2,1,0:T(8,128)(2,1)} custom-call(s32[1]{0:T(128)} %bitcast.2.scal, bf16[2,120,2560]{2,1,0:T(8,128)(2,1)} %bitcast.38, bf16[120,2560]{1,0:T(8,128)(2,1)} %stream.3, s32[1,120]{1,0:T(1,128)} %bitcast.48), custom_call_target="tpu_custom_call" | custom-call | tf_op jit(solution)/shard_map/pack/pallas_call | solution.py:133
  5.6 0.0 copy-start.9
  5.6 0.0 copy-start.7
  5.6 0.0 copy-start.8
  5.6 0.0 copy-start.10
  5.6 11.9 %all-to-all-start = ((bf16[64,320,128]{2,1,0:T(8,128)(2,1)}), bf16[64,320,128]{2,1,0:T(8,128)(2,1)}, u32[]{:S(2)}, u32[]{:S(2)}) async-start(bf16[64,320,128]{2,1,0:T(8,128)(2,1)} %pack.1), calls=%async_computation | async-start | bytes 10485760 | tf_op jit(solution)/shard_map/all_to_all | solution.py:540
  17.5 0.0 copy-done.9
  17.5 0.0 copy-done.7
  17.5 0.0 copy-done.8
  17.5 0.0 copy-start.3
  17.5 0.2 add_reduce_fusion
  17.8 3.2 %collective-permute-start = (f32[6,2560]{1,0:T(8,128)S(1)}, f32[6,2560]{1,0:T(8,128)S(1)}, u32[]{:S(2)}, u32[]{:S(2)}) collective-permute-start(f32[6,2560]{1,0:T(8,128)S(1)} %pad_maximum_fusion.1), channel_id=1, source_target_pairs={{0,32},{32,0},{1,33},{33,1},{2,34},{34,2},{3,35},{35,3},{4,36},{36... | collective-permute-start | bytes 184328 | tf_op jit(solution)/shard_map/ppermute | solution.py:535
  21.1 0.0 copy-done
  21.1 0.0 copy-done.10
  21.1 1.5 broadcast_add_fusion
  22.6 0.1 reshape.45
  22.7 12.8 %collective-permute-done = f32[6,2560]{1,0:T(8,128)S(1)} collective-permute-done((f32[6,2560]{1,0:T(8,128)S(1)}, f32[6,2560]{1,0:T(8,128)S(1)}, u32[]{:S(2)}, u32[]{:S(2)}) %collective-permute-start) | collective-permute-done | bytes 61472 | tf_op jit(solution)/shard_map/ppermute | solution.py:535
  35.5 0.0 copy-done.3
  35.7 0.6 copy.24
  36.3 0.6 slice_bitcast_fusion
  36.9 46.9 %all-to-all-done = bf16[64,320,128]{2,1,0:T(8,128)(2,1)} async-done(((bf16[64,320,128]{2,1,0:T(8,128)(2,1)}), bf16[64,320,128]{2,1,0:T(8,128)(2,1)}, u32[]{:S(2)}, u32[]{:S(2)}) %all-to-all-start) | async-done | bytes 5242912 | tf_op jit(solution)/shard_map/all_to_all | solution.py:540
  83.8 25.3 %first_layer.1 = (bf16[1280,128]{1,0:T(8,128)(2,1)}, bf16[64,64,128]{2,1,0:T(8,128)(2,1)}) custom-call(bf16[2,32,320,128]{3,2,1,0:T(8,128)(2,1)} %bitcast.5.kv.x_rest, bf16[2,32,320,128]{3,2,1,0:T(8,128)(2,1)} %bitcast.5.kv.x_rest, f32[16,384]{1,0:T(8,128)} %bitcast.45, f32[3,128]{1,0:T(4,128)} %get-tuple-element.14.maps), custom_call_target="tpu_custom_call" | custom-call | tf_op jit(solution)/shard_map/first_layer/pallas_call | solution.py:348
  109.1 0.0 copy-start.4
  109.1 11.4 %all-to-all-start.1 = ((bf16[64,64,128]{2,1,0:T(8,128)(2,1)}), bf16[64,64,128]{2,1,0:T(8,128)(2,1)S(1)}, u32[]{:S(2)}, u32[]{:S(2)}) async-start(bf16[64,64,128]{2,1,0:T(8,128)(2,1)} %get-tuple-element.5), calls=%async_computation.1 | async-start | bytes 2097152 | tf_op jit(solution)/shard_map/all_to_all | solution.py:566
  120.5 0.0 copy-done.4
  120.5 5.0 %collective-permute-start.1 = (bf16[1280,128]{1,0:T(8,128)(2,1)S(1)}, bf16[1280,128]{1,0:T(8,128)(2,1)S(1)}, u32[]{:S(2)}, u32[]{:S(2)}) collective-permute-start(bf16[1280,128]{1,0:T(8,128)(2,1)S(1)} %copy-done.4), channel_id=1, source_target_pairs={{1,0},{2,1},{0,2},{5,4},{6,5},{4,6},{9,8},{10,9},{8,10},{13,12},{1... | collective-permute-start | bytes 983048 | tf_op jit(solution)/shard_map/ppermute | solution.py:563
  125.5 1.9 collective-permute-start.2
  127.5 0.6 copy.23
  128.1 12.1 %collective-permute-done.1.after = bf16[1280,128]{1,0:T(8,128)(2,1)S(1)} collective-permute-done((bf16[1280,128]{1,0:T(8,128)(2,1)S(1)}, bf16[1280,128]{1,0:T(8,128)(2,1)S(1)}, u32[]{:S(2)}, u32[]{:S(2)}) %collective-permute-start.1) | collective-permute-done | bytes 327712 | tf_op jit(solution)/shard_map/ppermute | solution.py:563
  140.2 0.0 copy-start.5
  140.2 5.2 %collective-permute-done.2.before = bf16[1280,128]{1,0:T(8,128)(2,1)} collective-permute-done((bf16[1280,128]{1,0:T(8,128)(2,1)S(1)}, bf16[1280,128]{1,0:T(8,128)(2,1)}, u32[]{:S(2)}, u32[]{:S(2)}) %collective-permute-start.2) | collective-permute-done | bytes 327712 | tf_op jit(solution)/shard_map/ppermute | solution.py:563
  145.3 0.0 all-to-all-done.1.sums.got
  145.3 0.0 copy-start.1
  145.3 0.0 copy-done.5
  145.3 1.0 copy-done.1
  146.3 25.1 %second_layer.1.mine = bf16[1280,128]{1,0:T(8,128)(2,1)} custom-call(s32[1]{0:T(128)} %bitcast.1.scal, bf16[2,32,320,128]{3,2,1,0:T(8,128)(2,1)} %bitcast.5.kv.x_rest, bf16[1280,128]{1,0:T(8,128)(2,1)} %get-tuple-element.4.own, bf16[1280,128]{1,0:T(8,128)(2,1)} %copy-done.5, bf16[1280,128]{1,0:T(8,128)(2,1)} %collective-permute-done.2.before, ...), custom_call_target="tpu_custom_call" | custom-call | tf_op jit(solution)/shard_map/second_layer/pallas_call | solution.py:432
  171.4 0.0 collective-permute-start.3
  171.4 1.8 collective-permute-done.3.other
  173.3 0.0 copy-start.6
  173.3 0.7 copy-done.6
  174.0 3.3 %mix.1 = bf16[2,32,40,128]{3,2,1,0:T(8,128)(2,1)} custom-call(s32[1]{0:T(128)} %bitcast.scal, bf16[1280,128]{1,0:T(8,128)(2,1)} %second_layer.1.mine, bf16[1280,128]{1,0:T(8,128)(2,1)} %copy-done.6), custom_call_target="tpu_custom_call" | custom-call | tf_op jit(solution)/shard_map/mix/pallas_call | solution.py:493
  177.3 11.3 %all-to-all-start.2 = ((bf16[64,40,128]{2,1,0:T(8,128)(2,1)}), bf16[64,40,128]{2,1,0:T(8,128)(2,1)S(1)}, u32[]{:S(2)}, u32[]{:S(2)}) async-start(bf16[64,40,128]{2,1,0:T(8,128)(2,1)} %bitcast.36), calls=%async_computation.2 | async-start | bytes 1310720 | tf_op jit(solution)/shard_map/all_to_all | solution.py:573
  188.6 3.3 %home.1 = bf16[2,120,2560]{2,1,0:T(8,128)(2,1)} custom-call(s32[1]{0:T(128)} %bitcast.2.scal, bf16[64,64,128]{2,1,0:T(8,128)(2,1)} %copy-done.1, bf16[120,2560]{1,0:T(8,128)(2,1)} %stream.3, s32[1,120]{1,0:T(1,128)} %bitcast.49, f32[16,7680]{1,0:T(8,128)} %get-tuple-element.15.frame_mod, f32[3,2560]{1,0:T(4,128)} %bitcast.41), custom_call_target="tpu_custom_call" | custom-call | tf_op jit(solution)/shard_map/home/pallas_call | solution.py:466
  191.9 11.8 %all-to-all-done.2.got = bf16[64,40,128]{2,1,0:T(8,128)(2,1)S(1)} async-done(((bf16[64,40,128]{2,1,0:T(8,128)(2,1)}), bf16[64,40,128]{2,1,0:T(8,128)(2,1)S(1)}, u32[]{:S(2)}, u32[]{:S(2)}) %all-to-all-start.2) | async-done | bytes 655392 | tf_op jit(solution)/shard_map/all_to_all | solution.py:573
  203.6 0.0 copy-start.2
  203.6 0.8 copy-done.2
  204.5 1.9 unpack.1
  (17 shorter events, 0.3 us)
Async XLA Ops:
  0.6 20.4 %copy-start = (f32[50,7680]{1,0:T(8,128)S(1)}, f32[50,7680]{1,0:T(8,128)}, u32[]{:S(2)}) copy-start(f32[50,7680]{1,0:T(8,128)} %param.11) | copy-start | bytes 4608004
  5.6 11.9 %copy-start.9 = (f32[1,3,2560]{2,0,1:T(1,128)S(1)}, f32[1,3,2560]{2,0,1:T(1,128)}, u32[]{:S(2)}) copy-start(f32[1,3,2560]{2,0,1:T(1,128)} %param.14) | copy-start | bytes 92164
  5.6 11.9 %copy-start.7 = (f32[1,7680]{1,0:T(1,128)S(1)}, f32[1,7680]{1,0:T(1,128)}, u32[]{:S(2)}) copy-start(f32[1,7680]{1,0:T(1,128)} %param.13) | copy-start | bytes 92164
  5.6 11.9 %copy-start.8 = (f32[1,7680]{1,0:T(1,128)S(1)}, f32[1,7680]{1,0:T(1,128)}, u32[]{:S(2)}) copy-start(f32[1,7680]{1,0:T(1,128)} %param.12) | copy-start | bytes 92164
  5.6 15.5 %copy-start.10 = (s32[16]{0:T(128)S(1)}, s32[16]{0:T(128)}, u32[]{:S(2)}) copy-start(s32[16]{0:T(128)} %param.10) | copy-start | bytes 196
  5.6 78.2 %all-to-all-start = ((bf16[64,320,128]{2,1,0:T(8,128)(2,1)}), bf16[64,320,128]{2,1,0:T(8,128)(2,1)}, u32[]{:S(2)}, u32[]{:S(2)}) async-start(bf16[64,320,128]{2,1,0:T(8,128)(2,1)} %pack.1), calls=%async_computation | async-start | bytes 10485760 | tf_op jit(solution)/shard_map/all_to_all | solution.py:540
  17.5 18.0 %copy-start.3 = (f32[1,3,2560]{2,1,0:T(4,128)}, f32[1,3,2560]{2,1,0:T(4,128)S(1)}, u32[]{:S(2)}) copy-start(f32[1,3,2560]{2,1,0:T(4,128)S(1)} %copy.22) | copy-start | bytes 92164
  17.8 17.6 %collective-permute-start = (f32[6,2560]{1,0:T(8,128)S(1)}, f32[6,2560]{1,0:T(8,128)S(1)}, u32[]{:S(2)}, u32[]{:S(2)}) collective-permute-start(f32[6,2560]{1,0:T(8,128)S(1)} %pad_maximum_fusion.1), channel_id=1, source_target_pairs={{0,32},{32,0},{1,33},{33,1},{2,34},{34,2},{3,35},{35,3},{4,36},{36... | collective-permute-start | bytes 184328 | tf_op jit(solution)/shard_map/ppermute | solution.py:535
  109.1 11.4 %copy-start.4 = (bf16[1280,128]{1,0:T(8,128)(2,1)S(1)}, bf16[1280,128]{1,0:T(8,128)(2,1)}, u32[]{:S(2)}) copy-start(bf16[1280,128]{1,0:T(8,128)(2,1)} %get-tuple-element.4.own) | copy-start | bytes 983044
  109.1 36.2 %all-to-all-start.1 = ((bf16[64,64,128]{2,1,0:T(8,128)(2,1)}), bf16[64,64,128]{2,1,0:T(8,128)(2,1)S(1)}, u32[]{:S(2)}, u32[]{:S(2)}) async-start(bf16[64,64,128]{2,1,0:T(8,128)(2,1)} %get-tuple-element.5), calls=%async_computation.1 | async-start | bytes 2097152 | tf_op jit(solution)/shard_map/all_to_all | solution.py:566
  120.5 19.6 %collective-permute-start.1 = (bf16[1280,128]{1,0:T(8,128)(2,1)S(1)}, bf16[1280,128]{1,0:T(8,128)(2,1)S(1)}, u32[]{:S(2)}, u32[]{:S(2)}) collective-permute-start(bf16[1280,128]{1,0:T(8,128)(2,1)S(1)} %copy-done.4), channel_id=1, source_target_pairs={{1,0},{2,1},{0,2},{5,4},{6,5},{4,6},{9,8},{10,9},{8,10},{13,12},{1... | collective-permute-start | bytes 983048 | tf_op jit(solution)/shard_map/ppermute | solution.py:563
  125.5 19.8 %collective-permute-start.2 = (bf16[1280,128]{1,0:T(8,128)(2,1)S(1)}, bf16[1280,128]{1,0:T(8,128)(2,1)}, u32[]{:S(2)}, u32[]{:S(2)}) collective-permute-start(bf16[1280,128]{1,0:T(8,128)(2,1)S(1)} %copy-done.4), channel_id=1, source_target_pairs={{2,0},{0,1},{1,2},{6,4},{4,5},{5,6},{10,8},{8,9},{9,10},{14,12},{1... | collective-permute-start | bytes 983048 | tf_op jit(solution)/shard_map/ppermute | solution.py:563
  140.2 5.2 %copy-start.5 = (bf16[1280,128]{1,0:T(8,128)(2,1)}, bf16[1280,128]{1,0:T(8,128)(2,1)S(1)}, u32[]{:S(2)}) copy-start(bf16[1280,128]{1,0:T(8,128)(2,1)S(1)} %collective-permute-done.1.after) | copy-start | bytes 983044
  145.3 1.0 copy-start.1
  171.4 1.8 collective-permute-start.3
  173.3 0.7 copy-start.6
  177.3 26.3 %all-to-all-start.2 = ((bf16[64,40,128]{2,1,0:T(8,128)(2,1)}), bf16[64,40,128]{2,1,0:T(8,128)(2,1)S(1)}, u32[]{:S(2)}, u32[]{:S(2)}) async-start(bf16[64,40,128]{2,1,0:T(8,128)(2,1)} %bitcast.36), calls=%async_computation.2 | async-start | bytes 1310720 | tf_op jit(solution)/shard_map/all_to_all | solution.py:573
  203.6 0.8 copy-start.2
